TPU v7x, 32 devices: a whole 2x2x4 slice. The times are simulated.
32 devices in a mesh: ka: 4 (over x, core), brick: 8 (over z, y).
Axes of the slice: x: 2, y: 2, z: 4, core: 2. Of those that a mesh axis runs over, the one named last changes fastest.
Arguments:
- spinors: bfloat16 [32, 4, 32, 36864], P('ka', None, 'brick'), may hold values from -6 to 6
- kpt_mult: int32 [32], P('ka'), may hold values from 1 to 4
- occupied: int32 [32], P('ka'), may hold values 0 or 1
- core_density: float32 [32, 36864], P('brick'), may hold values from 0.05 to 1
- local_potential: float32 [32, 36864], P('brick'), may hold values from -6 to 6
Outputs:
- applied: bfloat16 [32, 4, 32, 36864], P('ka', None, 'brick')
All inputs are finite; a program needn't handle non-finite values. No bound on the sum of `occupied` on one device may be relied on, other than what follows from the above.
Results may differ from a plain program's by a relative error of at most 0.005.
Values may be sent and summed in bfloat16 or wider, within the bound.
No kernel may reach another device: no remote copies, remote signals or barrier semaphores. Data moves between devices by JAX's collectives and lax.ppermute only.
A program may use at most 128 MiB of HBM per device.

v0:
```python
import functools
import math

import jax
import jax.numpy as jnp
from jax import lax
from jax.experimental import pallas as pl
from jax.experimental.pallas import tpu as pltpu
from jax.sharding import PartitionSpec as P

NY = 192
LANES = 128
SUB = 8
TRIPLE = 3
HALF = 2 * NY - 2 * LANES - LANES // 2
PACK = 16
FLOOR_FRACTION = 0.05
VMEM_LIMIT = 63 * 1024 * 1024
SMALL = pl.CostEstimate(flops=0, bytes_accessed=0, transcendentals=0)


def rows_view(x):
    lead, planes, cells = x.shape[:-2], x.shape[-2], x.shape[-1]
    tiles = cells // LANES
    n = len(lead)
    x = x.reshape(lead + (planes, tiles, LANES))
    x = x.transpose(tuple(range(n)) + (n + 1, n, n + 2))
    return x.reshape(lead + (tiles * planes, LANES))


def planes_view(x, planes):
    lead, rows = x.shape[:-2], x.shape[-2]
    tiles = rows // planes
    n = len(lead)
    x = x.reshape(lead + (tiles, planes, LANES))
    x = x.transpose(tuple(range(n)) + (n + 1, n, n + 2))
    return x.reshape(lead + (planes, tiles * LANES))


def even_brick():
    return lax.axis_index("brick") % 2 == 0


def spread_matrix(back):
    size = SUB * PACK
    row = lax.broadcasted_iota(jnp.int32, (size, size), 0)
    column = lax.broadcasted_iota(jnp.int32, (size, size), 1)
    if back:
        row, column = column, row
    return (column == (row % SUB) * PACK + row // SUB).astype(jnp.bfloat16)


def gathered(read, segment, i):
    return jnp.concatenate(
        [read(pl.ds(s * segment + i * PACK, PACK)) for s in range(SUB)], axis=0
    )


def product(matrix, values):
    return jnp.dot(matrix, values, preferred_element_type=jnp.float32)


def face_matrix(planes):
    out = PACK // planes * SUB
    row = lax.broadcasted_iota(jnp.int32, (2 * out, SUB * PACK), 0)
    column = lax.broadcasted_iota(jnp.int32, (2 * out, SUB * PACK), 1)
    upper = (row < out) == even_brick()
    inner = row % out
    wanted = (inner % SUB) * PACK + (inner // SUB) * planes + jnp.where(upper, planes - 1, 0)
    return (column == wanted).astype(jnp.bfloat16), out


def edges_body(planes, chunks, x_ref, *refs):
    faces, held, sems = refs[-2 - 2 * len(chunks) : -2], refs[-2], refs[-1]
    first = chunks[0][0]
    bands = [(start - first + b, k, b) for k, (start, count) in enumerate(chunks) for b in range(count)]
    rows = held.shape[2]
    segment = rows // SUB
    copies = [pltpu.make_async_copy(x_ref.at[first + i], held.at[i], sems.at[i]) for i, _, _ in bands]
    for copy in copies:
        copy.start()
    select, out = face_matrix(planes)
    for i, k, b in bands:
        copies[i].wait()
        near_ref, far_ref = faces[2 * k], faces[2 * k + 1]
        for part in range(segment // PACK):
            block = jnp.concatenate(
                [gathered(lambda at: held[i, c, at, :], segment, part) for c in range(4)], axis=1
            )
            picked = product(select, block).astype(jnp.bfloat16)
            at = pl.ds(part * out, out)
            for c in range(4):
                lanes = slice(c * LANES, (c + 1) * LANES)
                near_ref[b, c, at, :] = picked[:out, lanes]
                far_ref[b, c, at, :] = picked[out:, lanes]


def edges(x, planes, chunks, after, limit):
    rows = x.shape[2]
    total = sum(count for _, count in chunks)
    shapes = [
        jax.ShapeDtypeStruct((count, 4, rows // planes, LANES), jnp.bfloat16) for _, count in chunks for _ in range(2)
    ]
    faces = pl.pallas_call(
        functools.partial(edges_body, planes, chunks),
        in_specs=[pl.BlockSpec(memory_space=pltpu.HBM)] + [pl.BlockSpec(memory_space=pl.ANY)] * len(after),
        out_shape=shapes,
        scratch_shapes=[pltpu.VMEM((total, 4, rows, LANES), jnp.bfloat16), pltpu.SemaphoreType.DMA((total,))],
        compiler_params=pltpu.CompilerParams(vmem_limit_bytes=limit),
        cost_estimate=SMALL,
        name="edges",
    )(x, *after)
    return [tuple(faces[2 * k : 2 * k + 2]) for k in range(len(chunks))]


def gate(near, far, after):
    anywhere = pl.BlockSpec(memory_space=pl.ANY)
    return pl.pallas_call(
        lambda *refs: None,
        in_specs=[anywhere] * (2 + len(after)),
        out_specs=[anywhere, anywhere],
        out_shape=[jax.ShapeDtypeStruct(a.shape, a.dtype) for a in (near, far)],
        input_output_aliases={0: 0, 1: 1},
        compiler_params=pltpu.CompilerParams(vmem_limit_bytes=VMEM_LIMIT),
        name="gate",
    )(near, far, *after)


def front_body(planes, scale, counts, mult_ref, occ_ref, x_ref, *refs):
    bands = x_ref.shape[0]
    density_ref, faces = refs[-1 - 2 * len(counts)], refs[len(refs) - 2 * len(counts) :]
    weights = [(mult_ref[b] * occ_ref[b]).astype(jnp.float32) * scale for b in range(bands)]
    for s in range(SUB):
        up = down = real = imag = None
        for b in range(bands):
            ur, ui, dr, di = (x_ref[b, c, s].astype(jnp.float32) for c in range(4))
            wur, wui = weights[b] * ur, weights[b] * ui
            wdr, wdi = weights[b] * dr, weights[b] * di
            terms = (
                wur * ur + wui * ui,
                wdr * dr + wdi * di,
                wur * dr + wui * di,
                wur * di - wui * dr,
            )
            if b == 0:
                up, down, real, imag = terms
            else:
                up, down, real, imag = up + terms[0], down + terms[1], real + terms[2], imag + terms[3]
        density_ref[0, s] = (up + down).astype(jnp.bfloat16)
        density_ref[1, s] = (2.0 * real).astype(jnp.bfloat16)
        density_ref[2, s] = (2.0 * imag).astype(jnp.bfloat16)
        density_ref[3, s] = (up - down).astype(jnp.bfloat16)
    if counts:
        select, out = face_matrix(planes)
    band = bands - sum(counts)
    for k, count in enumerate(counts):
        for b in range(count):
            block = jnp.concatenate(
                [x_ref[band, c].reshape(SUB * PACK, LANES) for c in range(4)], axis=1
            )
            picked = product(select, block).astype(jnp.bfloat16)
            for c in range(4):
                lanes = slice(c * LANES, (c + 1) * LANES)
                faces[2 * k][b, c] = picked[:out, lanes]
                faces[2 * k + 1][b, c] = picked[out:, lanes]
            band += 1


def front(x, mult, occ, total, planes, counts, after):
    bands, rows = x.shape[0], x.shape[2]
    segment = rows // SUB
    out = PACK // planes * SUB
    anywhere = pl.BlockSpec(memory_space=pl.ANY)
    results = pl.pallas_call(
        functools.partial(front_body, planes, 1.0 / (2.0 * total), counts),
        grid=(segment // PACK,),
        in_specs=[
            pl.BlockSpec(memory_space=pltpu.SMEM),
            pl.BlockSpec(memory_space=pltpu.SMEM),
            pl.BlockSpec((bands, 4, SUB, PACK, LANES), lambda i: (0, 0, 0, i, 0)),
        ]
        + [anywhere] * len(after),
        out_specs=[pl.BlockSpec((4, SUB, PACK, LANES), lambda i: (0, 0, i, 0))]
        + [pl.BlockSpec((count, 4, out, LANES), lambda i: (0, 0, i, 0)) for count in counts for _ in range(2)],
        out_shape=[jax.ShapeDtypeStruct((4, SUB, segment, LANES), jnp.bfloat16)]
        + [
            jax.ShapeDtypeStruct((count, 4, rows // planes, LANES), jnp.bfloat16)
            for count in counts
            for _ in range(2)
        ],
        compiler_params=pltpu.CompilerParams(vmem_limit_bytes=VMEM_LIMIT),
        cost_estimate=SMALL,
        name="front",
    )(mult, occ, x.reshape(bands, 4, SUB, segment, LANES), *after)
    return results[0].reshape(4, rows, LANES), [tuple(results[1 + 2 * k : 3 + 2 * k]) for k in range(len(counts))]


def cube_root(x):
    root = jnp.exp(jnp.log(jnp.abs(x)) * (1.0 / 3.0))
    return jnp.where(x < 0.0, -root, root)


def potential_body(rows, d_ref, core_ref, local_ref, out_ref):
    segment = rows // SUB
    spread = spread_matrix(False)

    def step(i, unused):
        block = jnp.concatenate([gathered(lambda at: d_ref[f, at, :], segment, i) for f in range(4)], axis=1)
        fields = product(spread, block)
        d0, d1, d2, d3 = (fields[:, f * LANES : (f + 1) * LANES] for f in range(4))
        here = [pl.ds(i * PACK + r, SUB, stride=segment) for r in range(PACK)]
        core = jnp.concatenate([core_ref[at, :] for at in here], axis=0)
        local = jnp.concatenate([local_ref[at, :] for at in here], axis=0)
        electrons = d0 + core
        magnitude = jnp.sqrt(d1 * d1 + d2 * d2 + d3 * d3)
        upper = -cube_root((3.0 / math.pi) * (electrons + magnitude))
        lower = -cube_root((3.0 / math.pi) * (electrons - magnitude))
        factor = 0.5 * (upper - lower) / jnp.maximum(magnitude, FLOOR_FRACTION * electrons)
        v = 0.5 * (upper + lower) + local
        bz = factor * d3
        at = pl.ds(i * PACK, PACK)
        shape = (PACK, SUB, LANES)
        out_ref[0, at] = (v + bz + 3.0).reshape(shape)
        out_ref[1, at] = (factor * d1).reshape(shape)
        out_ref[2, at] = (factor * d2).reshape(shape)
        out_ref[3, at] = (v - bz + 3.0).reshape(shape)
        return unused

    lax.fori_loop(0, segment // PACK, step, 0, unroll=True)


def potential_of(density, core, local):
    rows = density.shape[1]
    whole = pl.BlockSpec(memory_space=pltpu.VMEM)
    return pl.pallas_call(
        functools.partial(potential_body, rows),
        in_specs=[whole, whole, whole],
        out_specs=whole,
        out_shape=jax.ShapeDtypeStruct((4, rows // SUB, SUB, LANES), jnp.float32),
        compiler_params=pltpu.CompilerParams(vmem_limit_bytes=VMEM_LIMIT),
        cost_estimate=SMALL,
        name="potential",
    )(density, core, local)


def apply_body(planes, rows, x_ref, pot_ref, near_ref, far_ref, carry_ref, out_ref, token_ref, wide, ends, turned, flat):
    segment = rows // SUB
    stride = planes * TRIPLE
    steps = segment // stride
    near_slot = jnp.where(even_brick(), 1, 0)
    spread, unspread = spread_matrix(False), spread_matrix(True)

    for c in range(4):
        ends[near_slot, c] = near_ref[0, c].astype(jnp.float32).reshape(ends.shape[2:])
        ends[1 - near_slot, c] = far_ref[0, c].astype(jnp.float32).reshape(ends.shape[2:])

    def load(i, unused):
        block = jnp.concatenate([gathered(lambda at: x_ref[0, c, at, :], segment, i) for c in range(4)], axis=1)
        values = product(spread, block)
        for c in range(4):
            part = values[:, c * LANES : (c + 1) * LANES]
            wide[c, pl.ds(i * PACK, PACK)] = part.reshape(PACK, SUB, LANES)
            turned[c, pl.ds(stride + i * PACK, PACK)] = pltpu.roll(part, HALF, 1).reshape(PACK, SUB, LANES)
        return unused

    lax.fori_loop(0, segment // PACK, load, 0, unroll=True)
    for c in range(4):
        for q in range(stride):
            turned[c, q] = pltpu.roll(turned[c, segment + q], 1, 0)
            turned[c, segment + stride + q] = pltpu.roll(turned[c, stride + q], SUB - 1, 0)

    lane = lax.broadcasted_iota(jnp.int32, (SUB, LANES), 1)
    low = lane < HALF
    initial, final = lane == 0, lane == LANES - 1
    inner_initial, inner_final = lane == HALF, lane == HALF - 1

    def neighbours(c, plane, j):
        spot = [j * stride + tile * planes + plane for tile in range(TRIPLE)]
        v0, v1, v2 = (wide[c, at] for at in spot)
        r0, r1, r2 = (turned[c, at + stride] for at in spot)
        after0 = r0 + turned[c, spot[0] + 2 * stride]
        after1 = r1 + turned[c, spot[1] + 2 * stride]
        before1 = r1 + turned[c, spot[1]]
        before2 = r2 + turned[c, spot[2]]
        across = (
            jnp.where(low, before1, before2),
            jnp.where(low, before2, after0),
            jnp.where(low, after0, after1),
        )
        plus = (
            jnp.where(initial, v1, v0),
            jnp.where(inner_initial, r0, jnp.where(initial, v2, v1)),
            jnp.where(initial, r1, v2),
        )
        minus = (
            jnp.where(final, r1, v0),
            jnp.where(inner_final, r2, jnp.where(final, v0, v1)),
            jnp.where(final, v1, v2),
        )
        sums = []
        for tile in range(TRIPLE):
            below = ends[0, c, j * TRIPLE + tile] if plane == 0 else wide[c, spot[tile] - 1]
            above = ends[1, c, j * TRIPLE + tile] if plane == planes - 1 else wide[c, spot[tile] + 1]
            along = pltpu.roll(plus[tile], LANES - 1, 1) + pltpu.roll(minus[tile], 1, 1)
            sums.append((across[tile] + along) + (below + above))
        return (v0, v1, v2), sums

    def step(j, unused):
        for plane in range(planes):
            (ur, nur), (ui, nui), (dr, ndr), (di, ndi) = (neighbours(c, plane, j) for c in range(4))
            for tile in range(TRIPLE):
                spot = j * stride + tile * planes + plane
                diag_up, bx, by, diag_down = (pot_ref[f, spot] for f in range(4))
                a, b, e, f = ur[tile], ui[tile], dr[tile], di[tile]
                flat[0, spot] = diag_up * a + bx * e + by * f - 0.5 * nur[tile]
                flat[1, spot] = diag_up * b + bx * f - by * e - 0.5 * nui[tile]
                flat[2, spot] = bx * a - by * b + diag_down * e - 0.5 * ndr[tile]
                flat[3, spot] = bx * b + by * a + diag_down * f - 0.5 * ndi[tile]
        return unused

    lax.fori_loop(0, steps, step, 0)

    def store(i, unused):
        at = pl.ds(i * PACK, PACK)
        block = jnp.concatenate([flat[c, at].reshape(PACK * SUB, LANES) for c in range(4)], axis=1)
        values = product(unspread, block.astype(jnp.bfloat16)).astype(jnp.bfloat16)
        for c in range(4):
            for s in range(SUB):
                out_ref[0, c, pl.ds(pl.multiple_of(s * segment + i * PACK, PACK), PACK), :] = values[
                    s * PACK : (s + 1) * PACK, c * LANES : (c + 1) * LANES
                ]
        return unused

    lax.fori_loop(0, segment // PACK, store, 0, unroll=True)


def apply_bands(x, potential, near, far, planes, start, carry):
    count, rows = near.shape[0], x.shape[2]
    segment = rows // SUB
    stride = planes * TRIPLE
    tiles = rows // planes
    halo = pl.BlockSpec((1, 4, tiles, LANES), lambda b: (b, 0, 0, 0))
    body = functools.partial(apply_body, planes, rows)
    in_specs = [
        pl.BlockSpec((1, 4, rows, LANES), lambda b: (start + b, 0, 0, 0)),
        pl.BlockSpec((4, segment, SUB, LANES), lambda b: (0, 0, 0, 0)),
        halo,
        halo,
    ]
    operands = [x, potential, near, far]
    aliases = {}
    if carry is not None:
        in_specs.append(pl.BlockSpec(memory_space=pl.ANY))
        operands.append(carry)
        aliases = {4: 0}
        call = body
    else:

        def call(x_ref, pot_ref, near_ref, far_ref, *rest):
            body(x_ref, pot_ref, near_ref, far_ref, None, *rest)

    return pl.pallas_call(
        call,
        grid=(count,),
        in_specs=in_specs,
        out_specs=[
            pl.BlockSpec((1, 4, rows, LANES), lambda b: (start + b, 0, 0, 0)),
            pl.BlockSpec(memory_space=pl.ANY),
        ],
        out_shape=[
            jax.ShapeDtypeStruct(x.shape, jnp.bfloat16),
            jax.ShapeDtypeStruct((SUB, LANES), jnp.float32),
        ],
        input_output_aliases=aliases,
        scratch_shapes=[
            pltpu.VMEM((4, segment, SUB, LANES), jnp.float32),
            pltpu.VMEM((2, 4, tiles // SUB, SUB, LANES), jnp.float32),
            pltpu.VMEM((4, segment + 2 * stride, SUB, LANES), jnp.float32),
            pltpu.VMEM((4, segment, SUB, LANES), jnp.float32),
        ],
        compiler_params=pltpu.CompilerParams(vmem_limit_bytes=VMEM_LIMIT),
        cost_estimate=SMALL,
        name="apply",
    )(*operands)


def chunk_sizes(bands):
    return [2] * (bands // 2) + [1] * (bands % 2)


def shards(spinors, kpt_mult, occupied, core_density, local_potential):
    bands, planes = spinors.shape[0], spinors.shape[2]
    total = bands * lax.axis_size("ka")
    size = lax.axis_size("brick")
    near_pairs = [(i, i ^ 1) for i in range(size) if i ^ 1 < size]
    far_pairs = [(i, j) for i in range(size) for j in [((i + 1) ^ 1) - 1] if 0 <= j < size]
    x = rows_view(spinors)
    core, local = rows_view(core_density), rows_view(local_potential)
    sizes = chunk_sizes(bands)
    starts = [sum(sizes[:k]) for k in range(len(sizes))]

    swap = lambda face: (lax.ppermute(face[0], "brick", near_pairs), lax.ppermute(face[1], "brick", far_pairs))
    faces = edges(x, planes, [(0, sizes[0])], (), VMEM_LIMIT)
    halos = [swap(faces[0])]
    density, others = front(x, kpt_mult, occupied, total, planes, sizes[1:], faces[0][:1])
    faces += others
    halos += [swap(face) for face in faces[1:2]]
    potential = potential_of(lax.psum(density, "ka"), core, local)
    out, token = None, ()
    for k, start in enumerate(starts):
        if k + 2 < len(starts):
            halos.append(swap(gate(*faces[k + 2], halos[k] + token)))
        out, done = apply_bands(x, potential, *halos[k], planes, start, out)
        token = (done,)
    return planes_view(out, planes)


def solution(mesh):
    placed = (P("ka", None, "brick", None), P("ka"), P("ka"), P("brick", None), P("brick", None))
    return jax.shard_map(
        shards, mesh=mesh, in_specs=placed, out_specs=P("ka", None, "brick", None), check_vma=False
    )
```

profile of v0, /device:TPU:0, one launch (start us, length us, event | category | flops | bytes accessed | tf_op | source)
XLA Modules:
  0.0 132.0 jit_solution(393236320086095450)
XLA Ops:
  6.5 3.0 %edges.1 = (bf16[2,4,288,128]{3,2,1,0:T(8,128)(2,1)}, bf16[2,4,288,128]{3,2,1,0:T(8,128)(2,1)}) custom-call(bf16[8,4,1152,128]{3,2,1,0:T(8,128)(2,1)} %bitcast.23), custom_call_target="tpu_custom_call" | custom-call | tf_op jit(solution)/shard_map/edges/pallas_call | solution.py:104
  9.5 3.0 %collective-permute-start.2 = (bf16[2,4,288,128]{3,2,1,0:T(8,128)(2,1)}, bf16[2,4,288,128]{3,2,1,0:T(8,128)(2,1)}, u32[]{:S(2)}, u32[]{:S(2)}) collective-permute-start(bf16[2,4,288,128]{3,2,1,0:T(8,128)(2,1)} %get-tuple-element.23.refs_0_), channel_id=1, source_target_pairs={{0,1},{1,0},{2,3},{3,2},{4,5},{5,4},{6,7},{7,6},{8,9},{9,8},{10,11... | collective-permute-start | bytes 1769480 | tf_op jit(solution)/shard_map/ppermute | solution.py:402
  12.6 1.5 %collective-permute-start.3 = (bf16[2,4,288,128]{3,2,1,0:T(8,128)(2,1)}, bf16[2,4,288,128]{3,2,1,0:T(8,128)(2,1)}, u32[]{:S(2)}, u32[]{:S(2)}) collective-permute-start(bf16[2,4,288,128]{3,2,1,0:T(8,128)(2,1)} %get-tuple-element.29), channel_id=1, source_target_pairs={{1,2},{2,1},{3,4},{4,3},{5,6},{6,5},{9,10},{10,9},{11,12},{12,11},... | collective-permute-start | bytes 1769480 | tf_op jit(solution)/shard_map/ppermute | solution.py:402
  14.0 11.4 %front.1 = (bf16[4,8,144,128]{3,2,1,0:T(8,128)(2,1)}, bf16[2,4,288,128]{3,2,1,0:T(8,128)(2,1)}, bf16[2,4,288,128]{3,2,1,0:T(8,128)(2,1)}, bf16[2,4,288,128]{3,2,...) custom-call(s32[8]{0:T(128)} %mult_ref.1, ...), custom_call_target="tpu_custom_call" | custom-call | tf_op jit(solution)/shard_map/front/pallas_call | solution.py:174
  25.4 0.0 all-reduce.2.cloned.1.call-update
  25.4 3.6 %collective-permute-start = (bf16[2,4,288,128]{3,2,1,0:T(8,128)(2,1)}, bf16[2,4,288,128]{3,2,1,0:T(8,128)(2,1)S(1)}, u32[]{:S(2)}, u32[]{:S(2)}) collective-permute-start(bf16[2,4,288,128]{3,2,1,0:T(8,128)(2,1)} %get-tuple-element.27), channel_id=1, source_target_pairs={{0,1},{1,0},{2,3},{3,2},{4,5},{5,4},{6,7},{7,6},{8,9},{9,8},{10,11... | collective-permute-start | bytes 1769480 | tf_op jit(solution)/shard_map/ppermute | solution.py:402
  29.0 1.5 %collective-permute-start.1 = (bf16[2,4,288,128]{3,2,1,0:T(8,128)(2,1)}, bf16[2,4,288,128]{3,2,1,0:T(8,128)(2,1)}, u32[]{:S(2)}, u32[]{:S(2)}) collective-permute-start(bf16[2,4,288,128]{3,2,1,0:T(8,128)(2,1)} %get-tuple-element.28), channel_id=1, source_target_pairs={{1,2},{2,1},{3,4},{4,3},{5,6},{6,5},{9,10},{10,9},{11,12},{12,11},... | collective-permute-start | bytes 1769480 | tf_op jit(solution)/shard_map/ppermute | solution.py:402
  30.5 21.4 %collective-permute-done.2.near_ref.refs_2_ = bf16[2,4,288,128]{3,2,1,0:T(8,128)(2,1)} collective-permute-done((bf16[2,4,288,128]{3,2,1,0:T(8,128)(2,1)}, bf16[2,4,288,128]{3,2,1,0:T(8,128)(2,1)}, u32[]{:S(2)}, u32[]{:S(2)}) %collective-permute-start.2) | collective-permute-done | bytes 589856 | tf_op jit(solution)/shard_map/ppermute | solution.py:402
  51.9 2.5 %collective-permute-start.6 = (bf16[2,4,288,128]{3,2,1,0:T(8,128)(2,1)}, bf16[2,4,288,128]{3,2,1,0:T(8,128)(2,1)}, u32[]{:S(2)}, u32[]{:S(2)}) collective-permute-start(bf16[2,4,288,128]{3,2,1,0:T(8,128)(2,1)} %get-tuple-element.35), channel_id=1, source_target_pairs={{0,1},{1,0},{2,3},{3,2},{4,5},{5,4},{6,7},{7,6},{8,9},{9,8},{10,11... | collective-permute-start | bytes 1769480 | tf_op jit(solution)/shard_map/ppermute | solution.py:402
  54.4 1.5 %collective-permute-start.7 = (bf16[2,4,288,128]{3,2,1,0:T(8,128)(2,1)}, bf16[2,4,288,128]{3,2,1,0:T(8,128)(2,1)}, u32[]{:S(2)}, u32[]{:S(2)}) collective-permute-start(bf16[2,4,288,128]{3,2,1,0:T(8,128)(2,1)} %get-tuple-element.36), channel_id=1, source_target_pairs={{1,2},{2,1},{3,4},{4,3},{5,6},{6,5},{9,10},{10,9},{11,12},{12,11},... | collective-permute-start | bytes 1769480 | tf_op jit(solution)/shard_map/ppermute | solution.py:402
  55.8 9.2 %all-reduce.2.cloned.1.call-done.d_ref = bf16[4,1152,128]{2,1,0:T(8,128)(2,1)} async-done(((bf16[4,1152,128]{2,1,0:T(8,128)(2,1)}), bf16[4,1152,128]{2,1,0:T(8,128)(2,1)}) %all-reduce.2.cloned.1.call-update) | async-done | bytes 1179664 | tf_op jit(solution)/shard_map/psum | solution.py:408
  65.1 4.4 %potential.1.pot_ref = f32[4,144,8,128]{3,2,1,0:T(8,128)} custom-call(bf16[4,1152,128]{2,1,0:T(8,128)(2,1)} %all-reduce.2.cloned.1.call-done.d_ref, f32[1152,128]{1,0:T(8,128)} %bitcast.30, f32[1152,128]{1,0:T(8,128)} %bitcast.31), custom_call_target="tpu_custom_call" | custom-call | tf_op jit(solution)/shard_map/potential/pallas_call | solution.py:235
  69.5 10.3 %apply.4 = (bf16[8,4,1152,128]{3,2,1,0:T(8,128)(2,1)}, f32[8,128]{1,0:T(8,128)}) custom-call(bf16[8,4,1152,128]{3,2,1,0:T(8,128)(2,1)} %bitcast.25, f32[4,144,8,128]{3,2,1,0:T(8,128)} %potential.1.pot_ref, bf16[2,4,288,128]{3,2,1,0:T(8,128)(2,1)} %collective-permute-done.2.near_ref.refs_2_, bf16[2,4,288,128]{3,2,1,0:T(8,128)(2,1)} %collective-permute-done.3.far_ref.refs_3_), custom_call_target="tpu_custom_call" | custom-call | tf_op jit(solution)/shard_map/apply/pallas_call | solution.py:362
  79.9 0.0 collective-permute-done.refs_2_.near_ref
  79.9 0.8 copy-done
  80.7 1.5 %collective-permute-start.4 = (bf16[2,4,288,128]{3,2,1,0:T(8,128)(2,1)}, bf16[2,4,288,128]{3,2,1,0:T(8,128)(2,1)S(1)}, u32[]{:S(2)}, u32[]{:S(2)}) collective-permute-start(bf16[2,4,288,128]{3,2,1,0:T(8,128)(2,1)} %get-tuple-element.31), channel_id=1, source_target_pairs={{0,1},{1,0},{2,3},{3,2},{4,5},{5,4},{6,7},{7,6},{8,9},{9,8},{10,11... | collective-permute-start | bytes 1769480 | tf_op jit(solution)/shard_map/ppermute | solution.py:402
  82.2 1.5 %collective-permute-start.5 = (bf16[2,4,288,128]{3,2,1,0:T(8,128)(2,1)}, bf16[2,4,288,128]{3,2,1,0:T(8,128)(2,1)}, u32[]{:S(2)}, u32[]{:S(2)}) collective-permute-start(bf16[2,4,288,128]{3,2,1,0:T(8,128)(2,1)} %get-tuple-element.32), channel_id=1, source_target_pairs={{1,2},{2,1},{3,4},{4,3},{5,6},{6,5},{9,10},{10,9},{11,12},{12,11},... | collective-permute-start | bytes 1769480 | tf_op jit(solution)/shard_map/ppermute | solution.py:402
  83.7 10.3 %apply.5 = (bf16[8,4,1152,128]{3,2,1,0:T(8,128)(2,1)}, f32[8,128]{1,0:T(8,128)}) custom-call(bf16[8,4,1152,128]{3,2,1,0:T(8,128)(2,1)} %bitcast.26, f32[4,144,8,128]{3,2,1,0:T(8,128)} %potential.1.pot_ref, bf16[2,4,288,128]{3,2,1,0:T(8,128)(2,1)} %copy-done, ...), custom_call_target="tpu_custom_call", output_to_operand_aliasing={{0}: (4, {})} | custom-call | tf_op jit(solution)/shard_map/apply/pallas_call | solution.py:362
  94.0 8.4 %collective-permute-done.6.near_ref = bf16[2,4,288,128]{3,2,1,0:T(8,128)(2,1)} collective-permute-done((bf16[2,4,288,128]{3,2,1,0:T(8,128)(2,1)}, bf16[2,4,288,128]{3,2,1,0:T(8,128)(2,1)}, u32[]{:S(2)}, u32[]{:S(2)}) %collective-permute-start.6) | collective-permute-done | bytes 589856 | tf_op jit(solution)/shard_map/ppermute | solution.py:402
  102.4 10.3 %apply.6 = (bf16[8,4,1152,128]{3,2,1,0:T(8,128)(2,1)}, f32[8,128]{1,0:T(8,128)}) custom-call(bf16[8,4,1152,128]{3,2,1,0:T(8,128)(2,1)} %bitcast.27, f32[4,144,8,128]{3,2,1,0:T(8,128)} %potential.1.pot_ref, bf16[2,4,288,128]{3,2,1,0:T(8,128)(2,1)} %collective-permute-done.6.near_ref, ...), custom_call_target="tpu_custom_call", output_to_operand_aliasing={{0}: (4, {})} | custom-call | tf_op jit(solution)/shard_map/apply/pallas_call | solution.py:362
  112.8 1.1 collective-permute-done.4.near_ref
  113.9 0.0 collective-permute-done.5.far_ref
  113.9 0.8 copy-done.1
  114.8 10.3 %apply.7 = (bf16[8,4,1152,128]{3,2,1,0:T(8,128)(2,1)}, f32[8,128]{1,0:T(8,128)}) custom-call(bf16[8,4,1152,128]{3,2,1,0:T(8,128)(2,1)} %bitcast.28, f32[4,144,8,128]{3,2,1,0:T(8,128)} %potential.1.pot_ref, bf16[2,4,288,128]{3,2,1,0:T(8,128)(2,1)} %copy-done.1, ...), custom_call_target="tpu_custom_call", output_to_operand_aliasing={{0}: (4, {})} | custom-call | tf_op jit(solution)/shard_map/apply/pallas_call | solution.py:362
  (8 shorter events, 0.0 us)
Async XLA Ops:
  6.5 58.6 %all-reduce.2.cloned.1.call-start = ((), (), s32[]{:S(2)}) async-start(), calls=%async_computation | async-start | bytes 2359296 | tf_op jit(solution)/shard_map/psum | solution.py:408
  9.5 42.4 %collective-permute-start.2 = (bf16[2,4,288,128]{3,2,1,0:T(8,128)(2,1)}, bf16[2,4,288,128]{3,2,1,0:T(8,128)(2,1)}, u32[]{:S(2)}, u32[]{:S(2)}) collective-permute-start(bf16[2,4,288,128]{3,2,1,0:T(8,128)(2,1)} %get-tuple-element.23.refs_0_), channel_id=1, source_target_pairs={{0,1},{1,0},{2,3},{3,2},{4,5},{5,4},{6,7},{7,6},{8,9},{9,8},{10,11... | collective-permute-start | bytes 1769480 | tf_op jit(solution)/shard_map/ppermute | solution.py:402
  12.6 39.3 %collective-permute-start.3 = (bf16[2,4,288,128]{3,2,1,0:T(8,128)(2,1)}, bf16[2,4,288,128]{3,2,1,0:T(8,128)(2,1)}, u32[]{:S(2)}, u32[]{:S(2)}) collective-permute-start(bf16[2,4,288,128]{3,2,1,0:T(8,128)(2,1)} %get-tuple-element.29), channel_id=1, source_target_pairs={{1,2},{2,1},{3,4},{4,3},{5,6},{6,5},{9,10},{10,9},{11,12},{12,11},... | collective-permute-start | bytes 1769480 | tf_op jit(solution)/shard_map/ppermute | solution.py:402
  25.4 54.4 %collective-permute-start = (bf16[2,4,288,128]{3,2,1,0:T(8,128)(2,1)}, bf16[2,4,288,128]{3,2,1,0:T(8,128)(2,1)S(1)}, u32[]{:S(2)}, u32[]{:S(2)}) collective-permute-start(bf16[2,4,288,128]{3,2,1,0:T(8,128)(2,1)} %get-tuple-element.27), channel_id=1, source_target_pairs={{0,1},{1,0},{2,3},{3,2},{4,5},{5,4},{6,7},{7,6},{8,9},{9,8},{10,11... | collective-permute-start | bytes 1769480 | tf_op jit(solution)/shard_map/ppermute | solution.py:402
  29.0 50.9 %collective-permute-start.1 = (bf16[2,4,288,128]{3,2,1,0:T(8,128)(2,1)}, bf16[2,4,288,128]{3,2,1,0:T(8,128)(2,1)}, u32[]{:S(2)}, u32[]{:S(2)}) collective-permute-start(bf16[2,4,288,128]{3,2,1,0:T(8,128)(2,1)} %get-tuple-element.28), channel_id=1, source_target_pairs={{1,2},{2,1},{3,4},{4,3},{5,6},{6,5},{9,10},{10,9},{11,12},{12,11},... | collective-permute-start | bytes 1769480 | tf_op jit(solution)/shard_map/ppermute | solution.py:402
  51.9 50.6 %collective-permute-start.6 = (bf16[2,4,288,128]{3,2,1,0:T(8,128)(2,1)}, bf16[2,4,288,128]{3,2,1,0:T(8,128)(2,1)}, u32[]{:S(2)}, u32[]{:S(2)}) collective-permute-start(bf16[2,4,288,128]{3,2,1,0:T(8,128)(2,1)} %get-tuple-element.35), channel_id=1, source_target_pairs={{0,1},{1,0},{2,3},{3,2},{4,5},{5,4},{6,7},{7,6},{8,9},{9,8},{10,11... | collective-permute-start | bytes 1769480 | tf_op jit(solution)/shard_map/ppermute | solution.py:402
  54.4 48.1 %collective-permute-start.7 = (bf16[2,4,288,128]{3,2,1,0:T(8,128)(2,1)}, bf16[2,4,288,128]{3,2,1,0:T(8,128)(2,1)}, u32[]{:S(2)}, u32[]{:S(2)}) collective-permute-start(bf16[2,4,288,128]{3,2,1,0:T(8,128)(2,1)} %get-tuple-element.36), channel_id=1, source_target_pairs={{1,2},{2,1},{3,4},{4,3},{5,6},{6,5},{9,10},{10,9},{11,12},{12,11},... | collective-permute-start | bytes 1769480 | tf_op jit(solution)/shard_map/ppermute | solution.py:402
  79.9 0.8 copy-start
  80.7 33.2 %collective-permute-start.4 = (bf16[2,4,288,128]{3,2,1,0:T(8,128)(2,1)}, bf16[2,4,288,128]{3,2,1,0:T(8,128)(2,1)S(1)}, u32[]{:S(2)}, u32[]{:S(2)}) collective-permute-start(bf16[2,4,288,128]{3,2,1,0:T(8,128)(2,1)} %get-tuple-element.31), channel_id=1, source_target_pairs={{0,1},{1,0},{2,3},{3,2},{4,5},{5,4},{6,7},{7,6},{8,9},{9,8},{10,11... | collective-permute-start | bytes 1769480 | tf_op jit(solution)/shard_map/ppermute | solution.py:402
  82.2 31.8 %collective-permute-start.5 = (bf16[2,4,288,128]{3,2,1,0:T(8,128)(2,1)}, bf16[2,4,288,128]{3,2,1,0:T(8,128)(2,1)}, u32[]{:S(2)}, u32[]{:S(2)}) collective-permute-start(bf16[2,4,288,128]{3,2,1,0:T(8,128)(2,1)} %get-tuple-element.32), channel_id=1, source_target_pairs={{1,2},{2,1},{3,4},{4,3},{5,6},{6,5},{9,10},{10,9},{11,12},{12,11},... | collective-permute-start | bytes 1769480 | tf_op jit(solution)/shard_map/ppermute | solution.py:402
  113.9 0.8 copy-start.1
Sparse Core Ops, SparseCore 0:
  25.6 39.4 all-reduce.1
where the time goes:
time: 132 us
  Pallas kernels  60.2 us (46%)
  waiting for transfers between devices  40.3 us (31%)
  starting transfers between devices  16.5 us (12%)
  between operations  13.4 us (10%)
  local copies, waits for them, and re-layouts  1.64 us (1%)
    pallas_call x4, Pallas kernels, apply_bands(): pl.pallas_call(call, grid=(count,), in_specs=in_specs, out_specs=[pl.Bloc...  41.4 us
    ppermute x4, waiting for transfers between devices, shards(): lax.ppermute(face[0], 'brick', near_pairs)  31 us
    pallas_call x1, Pallas kernels, front(): pl.pallas_call(functools.partial(front_body, planes, 1.0 / (2.0 * total),...  11.4 us
    ppermute x4, starting transfers between devices, shards(): lax.ppermute(face[0], 'brick', near_pairs)  10.6 us
    psum x1, waiting for transfers between devices, shards(): potential = potential_of(lax.psum(density, 'ka'), core, local)  9.24 us
    ppermute x4, starting transfers between devices, shards(): lax.ppermute(face[1], 'brick', far_pairs)  5.9 us
    pallas_call x1, Pallas kernels, potential_of(): pl.pallas_call(functools.partial(potential_body, rows), in_specs=[whole,...  4.43 us
    pallas_call x1, Pallas kernels, edges(): pl.pallas_call(functools.partial(edges_body, planes, chunks), in_specs=[p...  2.97 us
  transfers between devices with their start and end apart: 9, of which 4 were waited for; matrix products, arithmetic and copies ran while one was open for 0% of the time, Pallas kernels for 35%

commit v1 on v0

--- a/solution.py
+++ b/solution.py
@@ -68,49 +68,6 @@
     inner = row % out
     wanted = (inner % SUB) * PACK + (inner // SUB) * planes + jnp.where(upper, planes - 1, 0)
     return (column == wanted).astype(jnp.bfloat16), out
-
-
-def edges_body(planes, chunks, x_ref, *refs):
-    faces, held, sems = refs[-2 - 2 * len(chunks) : -2], refs[-2], refs[-1]
-    first = chunks[0][0]
-    bands = [(start - first + b, k, b) for k, (start, count) in enumerate(chunks) for b in range(count)]
-    rows = held.shape[2]
-    segment = rows // SUB
-    copies = [pltpu.make_async_copy(x_ref.at[first + i], held.at[i], sems.at[i]) for i, _, _ in bands]
-    for copy in copies:
-        copy.start()
-    select, out = face_matrix(planes)
-    for i, k, b in bands:
-        copies[i].wait()
-        near_ref, far_ref = faces[2 * k], faces[2 * k + 1]
-        for part in range(segment // PACK):
-            block = jnp.concatenate(
-                [gathered(lambda at: held[i, c, at, :], segment, part) for c in range(4)], axis=1
-            )
-            picked = product(select, block).astype(jnp.bfloat16)
-            at = pl.ds(part * out, out)
-            for c in range(4):
-                lanes = slice(c * LANES, (c + 1) * LANES)
-                near_ref[b, c, at, :] = picked[:out, lanes]
-                far_ref[b, c, at, :] = picked[out:, lanes]
-
-
-def edges(x, planes, chunks, after, limit):
-    rows = x.shape[2]
-    total = sum(count for _, count in chunks)
-    shapes = [
-        jax.ShapeDtypeStruct((count, 4, rows // planes, LANES), jnp.bfloat16) for _, count in chunks for _ in range(2)
-    ]
-    faces = pl.pallas_call(
-        functools.partial(edges_body, planes, chunks),
-        in_specs=[pl.BlockSpec(memory_space=pltpu.HBM)] + [pl.BlockSpec(memory_space=pl.ANY)] * len(after),
-        out_shape=shapes,
-        scratch_shapes=[pltpu.VMEM((total, 4, rows, LANES), jnp.bfloat16), pltpu.SemaphoreType.DMA((total,))],
-        compiler_params=pltpu.CompilerParams(vmem_limit_bytes=limit),
-        cost_estimate=SMALL,
-        name="edges",
-    )(x, *after)
-    return [tuple(faces[2 * k : 2 * k + 2]) for k in range(len(chunks))]
 
 
 def gate(near, far, after):
@@ -150,9 +107,8 @@
         density_ref[1, s] = (2.0 * real).astype(jnp.bfloat16)
         density_ref[2, s] = (2.0 * imag).astype(jnp.bfloat16)
         density_ref[3, s] = (up - down).astype(jnp.bfloat16)
-    if counts:
-        select, out = face_matrix(planes)
-    band = bands - sum(counts)
+    select, out = face_matrix(planes)
+    band = 0
     for k, count in enumerate(counts):
         for b in range(count):
             block = jnp.concatenate(
@@ -166,11 +122,10 @@
             band += 1
 
 
-def front(x, mult, occ, total, planes, counts, after):
+def front(x, mult, occ, total, planes, counts):
     bands, rows = x.shape[0], x.shape[2]
     segment = rows // SUB
     out = PACK // planes * SUB
-    anywhere = pl.BlockSpec(memory_space=pl.ANY)
     results = pl.pallas_call(
         functools.partial(front_body, planes, 1.0 / (2.0 * total), counts),
         grid=(segment // PACK,),
@@ -178,8 +133,7 @@
             pl.BlockSpec(memory_space=pltpu.SMEM),
             pl.BlockSpec(memory_space=pltpu.SMEM),
             pl.BlockSpec((bands, 4, SUB, PACK, LANES), lambda i: (0, 0, 0, i, 0)),
-        ]
-        + [anywhere] * len(after),
+        ],
         out_specs=[pl.BlockSpec((4, SUB, PACK, LANES), lambda i: (0, 0, i, 0))]
         + [pl.BlockSpec((count, 4, out, LANES), lambda i: (0, 0, i, 0)) for count in counts for _ in range(2)],
         out_shape=[jax.ShapeDtypeStruct((4, SUB, segment, LANES), jnp.bfloat16)]
@@ -191,8 +145,25 @@
         compiler_params=pltpu.CompilerParams(vmem_limit_bytes=VMEM_LIMIT),
         cost_estimate=SMALL,
         name="front",
-    )(mult, occ, x.reshape(bands, 4, SUB, segment, LANES), *after)
+    )(mult, occ, x.reshape(bands, 4, SUB, segment, LANES))
     return results[0].reshape(4, rows, LANES), [tuple(results[1 + 2 * k : 3 + 2 * k]) for k in range(len(counts))]
+
+
+def add_body(a_ref, b_ref, *refs):
+    out_ref = refs[-1]
+    out_ref[...] = (a_ref[...].astype(jnp.float32) + b_ref[...].astype(jnp.float32)).astype(jnp.bfloat16)
+
+
+def add(a, b, after):
+    whole = pl.BlockSpec(memory_space=pltpu.VMEM)
+    return pl.pallas_call(
+        add_body,
+        in_specs=[whole, whole] + [pl.BlockSpec(memory_space=pl.ANY)] * len(after),
+        out_shape=jax.ShapeDtypeStruct(a.shape, a.dtype),
+        compiler_params=pltpu.CompilerParams(vmem_limit_bytes=VMEM_LIMIT),
+        cost_estimate=SMALL,
+        name="add",
+    )(a, b, *after)
 
 
 def cube_root(x):
@@ -200,14 +171,20 @@
     return jnp.where(x < 0.0, -root, root)
 
 
-def potential_body(rows, d_ref, core_ref, local_ref, out_ref):
+def potential_body(rows, d_ref, e_ref, core_ref, local_ref, out_ref):
     segment = rows // SUB
     spread = spread_matrix(False)
 
     def step(i, unused):
-        block = jnp.concatenate([gathered(lambda at: d_ref[f, at, :], segment, i) for f in range(4)], axis=1)
+        block = jnp.concatenate(
+            [gathered(lambda at: d_ref[f, at, :], segment, i) for f in range(4)]
+            + [gathered(lambda at: e_ref[f, at, :], segment, i) for f in range(4)],
+            axis=1,
+        )
         fields = product(spread, block)
-        d0, d1, d2, d3 = (fields[:, f * LANES : (f + 1) * LANES] for f in range(4))
+        d0, d1, d2, d3 = (
+            fields[:, f * LANES : (f + 1) * LANES] + fields[:, (f + 4) * LANES : (f + 5) * LANES] for f in range(4)
+        )
         here = [pl.ds(i * PACK + r, SUB, stride=segment) for r in range(PACK)]
         core = jnp.concatenate([core_ref[at, :] for at in here], axis=0)
         local = jnp.concatenate([local_ref[at, :] for at in here], axis=0)
@@ -229,18 +206,18 @@
     lax.fori_loop(0, segment // PACK, step, 0, unroll=True)
 
 
-def potential_of(density, core, local):
+def potential_of(density, other, core, local):
     rows = density.shape[1]
     whole = pl.BlockSpec(memory_space=pltpu.VMEM)
     return pl.pallas_call(
         functools.partial(potential_body, rows),
-        in_specs=[whole, whole, whole],
+        in_specs=[whole, whole, whole, whole],
         out_specs=whole,
         out_shape=jax.ShapeDtypeStruct((4, rows // SUB, SUB, LANES), jnp.float32),
         compiler_params=pltpu.CompilerParams(vmem_limit_bytes=VMEM_LIMIT),
         cost_estimate=SMALL,
         name="potential",
-    )(density, core, local)
+    )(density, other, core, local)
 
 
 def apply_body(planes, rows, x_ref, pot_ref, near_ref, far_ref, carry_ref, out_ref, token_ref, wide, ends, turned, flat):
@@ -388,6 +365,20 @@
     return [2] * (bands // 2) + [1] * (bands % 2)
 
 
+def group_sum(partial, after):
+    size = lax.axis_size("ka")
+    if size & (size - 1) or size == 1:
+        whole = lax.psum(partial, "ka")
+        return whole, jnp.zeros_like(whole)
+    step = 1
+    while True:
+        other = lax.ppermute(partial, "ka", [(i, i ^ step) for i in range(size)])
+        step *= 2
+        if step == size:
+            return partial, other
+        partial = add(partial, other, after)
+
+
 def shards(spinors, kpt_mult, occupied, core_density, local_potential):
     bands, planes = spinors.shape[0], spinors.shape[2]
     total = bands * lax.axis_size("ka")
@@ -400,12 +391,10 @@
     starts = [sum(sizes[:k]) for k in range(len(sizes))]
 
     swap = lambda face: (lax.ppermute(face[0], "brick", near_pairs), lax.ppermute(face[1], "brick", far_pairs))
-    faces = edges(x, planes, [(0, sizes[0])], (), VMEM_LIMIT)
-    halos = [swap(faces[0])]
-    density, others = front(x, kpt_mult, occupied, total, planes, sizes[1:], faces[0][:1])
-    faces += others
-    halos += [swap(face) for face in faces[1:2]]
-    potential = potential_of(lax.psum(density, "ka"), core, local)
+    density, faces = front(x, kpt_mult, occupied, total, planes, sizes)
+    halos = [swap(face) for face in faces[:2]]
+    own, other = group_sum(density, ())
+    potential = potential_of(own, other, core, local)
     out, token = None, ()
     for k, start in enumerate(starts):
         if k + 2 < len(starts):

time: 132 us -> 136 us (1.030)
  between operations: 13.4 us -> 0.02 us
  waiting for transfers between devices: 40.3 us -> 53.1 us
  starting transfers between devices: 16.5 us -> 19.2 us
    ppermute x4, waiting for transfers between devices: 31 us -> 50.2 us  [shards(): lax.ppermute(face[0], 'brick', near_pairs)]
    psum x1 -> x0, waiting for transfers between devices: 9.24 us -> none  [shards(): potential = potential_of(lax.psum(density, 'ka'), core, local)]
    ppermute x0 -> x2, starting transfers between devices: none -> 3.37 us  [group_sum(): other = lax.ppermute(partial, 'ka', [(i, i ^ step) for i in range(size)])]
    ppermute x0 -> x2, waiting for transfers between devices: none -> 2.82 us  [group_sum(): other = lax.ppermute(partial, 'ka', [(i, i ^ step) for i in range(size)])]
  transfers between devices with their start and end apart: 9 -> 10, of which waited for: 4 -> 5; matrix products, arithmetic and copies ran while one was open for 0% -> 0% of each run, Pallas kernels for 35% -> 27%
where the time goes in v1:
time: 136 us; the launch traced here: 135 us
  Pallas kernels  61.1 us (45%)
  waiting for transfers between devices  53.1 us (39%)
  starting transfers between devices  19.2 us (14%)
  local copies, waits for them, and re-layouts  1.65 us (1%)
    ppermute x4, waiting for transfers between devices, shards(): lax.ppermute(face[0], 'brick', near_pairs)  50.2 us
    pallas_call x4, Pallas kernels, apply_bands(): pl.pallas_call(call, grid=(count,), in_specs=in_specs, out_specs=[pl.Bloc...  41.4 us
    pallas_call x1, Pallas kernels, front(): pl.pallas_call(functools.partial(front_body, planes, 1.0 / (2.0 * total),...  11.8 us
    ppermute x4, starting transfers between devices, shards(): lax.ppermute(face[0], 'brick', near_pairs)  9.89 us
    ppermute x4, starting transfers between devices, shards(): lax.ppermute(face[1], 'brick', far_pairs)  5.96 us
    pallas_call x1, Pallas kernels, potential_of(): pl.pallas_call(functools.partial(potential_body, rows), in_specs=[whole,...  4.97 us
    ppermute x2, starting transfers between devices, group_sum(): other = lax.ppermute(partial, 'ka', [(i, i ^ step) for i in range(size)])  3.37 us
    pallas_call x1, Pallas kernels, add(): pl.pallas_call(add_body, in_specs=[whole, whole] + [pl.BlockSpec(memory_s...  2.95 us
  transfers between devices with their start and end apart: 10, of which 5 were waited for; matrix products, arithmetic and copies ran while one was open for 0% of the time, Pallas kernels for 27%

profile of v1, /device:TPU:0, one launch (start us, length us, event | category | flops | bytes accessed | tf_op | source)
XLA Modules:
  0.0 135.1 jit_solution(5941709481690155521)
XLA Ops:
  0.0 11.8 %front.1 = (bf16[4,8,144,128]{3,2,1,0:T(8,128)(2,1)}, bf16[2,4,288,128]{3,2,1,0:T(8,128)(2,1)}, bf16[2,4,288,128]{3,2,1,0:T(8,128)(2,1)}, bf16[2,4,288,128]{3,2,...) custom-call(s32[8]{0:T(128)} %mult_ref.1, ...), custom_call_target="tpu_custom_call" | custom-call | tf_op jit(solution)/shard_map/front/pallas_call | solution.py:129
  11.8 0.5 collective-permute-start
  12.3 2.8 %collective-permute-done.b_ref = bf16[4,1152,128]{2,1,0:T(8,128)(2,1)} collective-permute-done((bf16[4,1152,128]{2,1,0:T(8,128)(2,1)}, bf16[4,1152,128]{2,1,0:T(8,128)(2,1)}, u32[]{:S(2)}, u32[]{:S(2)}) %collective-permute-start) | collective-permute-done | bytes 1179680 | tf_op jit(solution)/shard_map/ppermute | solution.py:375
  15.1 2.9 %add.1.d_ref = bf16[4,1152,128]{2,1,0:T(8,128)(2,1)} custom-call(bf16[4,1152,128]{2,1,0:T(8,128)(2,1)} %bitcast.29, bf16[4,1152,128]{2,1,0:T(8,128)(2,1)} %collective-permute-done.b_ref), custom_call_target="tpu_custom_call" | custom-call | tf_op jit(solution)/shard_map/add/pallas_call | solution.py:159
  18.1 2.9 %collective-permute-start.1 = (bf16[4,1152,128]{2,1,0:T(8,128)(2,1)}, bf16[4,1152,128]{2,1,0:T(8,128)(2,1)}, u32[]{:S(2)}, u32[]{:S(2)}) collective-permute-start(bf16[4,1152,128]{2,1,0:T(8,128)(2,1)} %add.1.d_ref), channel_id=1, source_target_pairs={{0,16},{8,24},{16,0},{24,8},{1,17},{9,25},{17,1},{25,9},{2,18},{10... | collective-permute-start | bytes 3538952 | tf_op jit(solution)/shard_map/ppermute | solution.py:375
  21.0 1.5 %collective-permute-start.4 = (bf16[2,4,288,128]{3,2,1,0:T(8,128)(2,1)}, bf16[2,4,288,128]{3,2,1,0:T(8,128)(2,1)}, u32[]{:S(2)}, u32[]{:S(2)}) collective-permute-start(bf16[2,4,288,128]{3,2,1,0:T(8,128)(2,1)} %get-tuple-element.28), channel_id=1, source_target_pairs={{0,1},{1,0},{2,3},{3,2},{4,5},{5,4},{6,7},{7,6},{8,9},{9,8},{10,11... | collective-permute-start | bytes 1769480 | tf_op jit(solution)/shard_map/ppermute | solution.py:393
  22.5 1.5 %collective-permute-start.5 = (bf16[2,4,288,128]{3,2,1,0:T(8,128)(2,1)}, bf16[2,4,288,128]{3,2,1,0:T(8,128)(2,1)}, u32[]{:S(2)}, u32[]{:S(2)}) collective-permute-start(bf16[2,4,288,128]{3,2,1,0:T(8,128)(2,1)} %get-tuple-element.29), channel_id=1, source_target_pairs={{1,2},{2,1},{3,4},{4,3},{5,6},{6,5},{9,10},{10,9},{11,12},{12,11},... | collective-permute-start | bytes 1769480 | tf_op jit(solution)/shard_map/ppermute | solution.py:393
  24.0 3.5 %collective-permute-start.2 = (bf16[2,4,288,128]{3,2,1,0:T(8,128)(2,1)}, bf16[2,4,288,128]{3,2,1,0:T(8,128)(2,1)S(1)}, u32[]{:S(2)}, u32[]{:S(2)}) collective-permute-start(bf16[2,4,288,128]{3,2,1,0:T(8,128)(2,1)} %get-tuple-element.26), channel_id=1, source_target_pairs={{0,1},{1,0},{2,3},{3,2},{4,5},{5,4},{6,7},{7,6},{8,9},{9,8},{10,11... | collective-permute-start | bytes 1769480 | tf_op jit(solution)/shard_map/ppermute | solution.py:393
  27.5 1.5 %collective-permute-start.3 = (bf16[2,4,288,128]{3,2,1,0:T(8,128)(2,1)}, bf16[2,4,288,128]{3,2,1,0:T(8,128)(2,1)}, u32[]{:S(2)}, u32[]{:S(2)}) collective-permute-start(bf16[2,4,288,128]{3,2,1,0:T(8,128)(2,1)} %get-tuple-element.27), channel_id=1, source_target_pairs={{1,2},{2,1},{3,4},{4,3},{5,6},{6,5},{9,10},{10,9},{11,12},{12,11},... | collective-permute-start | bytes 1769480 | tf_op jit(solution)/shard_map/ppermute | solution.py:393
  28.9 32.9 %collective-permute-done.4.near_ref.refs_2_ = bf16[2,4,288,128]{3,2,1,0:T(8,128)(2,1)} collective-permute-done((bf16[2,4,288,128]{3,2,1,0:T(8,128)(2,1)}, bf16[2,4,288,128]{3,2,1,0:T(8,128)(2,1)}, u32[]{:S(2)}, u32[]{:S(2)}) %collective-permute-start.4) | collective-permute-done | bytes 589856 | tf_op jit(solution)/shard_map/ppermute | solution.py:393
  61.8 2.5 %collective-permute-start.8 = (bf16[2,4,288,128]{3,2,1,0:T(8,128)(2,1)}, bf16[2,4,288,128]{3,2,1,0:T(8,128)(2,1)}, u32[]{:S(2)}, u32[]{:S(2)}) collective-permute-start(bf16[2,4,288,128]{3,2,1,0:T(8,128)(2,1)} %get-tuple-element.35), channel_id=1, source_target_pairs={{0,1},{1,0},{2,3},{3,2},{4,5},{5,4},{6,7},{7,6},{8,9},{9,8},{10,11... | collective-permute-start | bytes 1769480 | tf_op jit(solution)/shard_map/ppermute | solution.py:393
  64.3 1.5 %collective-permute-start.9 = (bf16[2,4,288,128]{3,2,1,0:T(8,128)(2,1)}, bf16[2,4,288,128]{3,2,1,0:T(8,128)(2,1)}, u32[]{:S(2)}, u32[]{:S(2)}) collective-permute-start(bf16[2,4,288,128]{3,2,1,0:T(8,128)(2,1)} %get-tuple-element.36), channel_id=1, source_target_pairs={{1,2},{2,1},{3,4},{4,3},{5,6},{6,5},{9,10},{10,9},{11,12},{12,11},... | collective-permute-start | bytes 1769480 | tf_op jit(solution)/shard_map/ppermute | solution.py:393
  65.8 5.0 %potential.1.pot_ref = f32[4,144,8,128]{3,2,1,0:T(8,128)} custom-call(bf16[4,1152,128]{2,1,0:T(8,128)(2,1)} %add.1.d_ref, bf16[4,1152,128]{2,1,0:T(8,128)(2,1)} %collective-permute-done.1.e_ref, f32[1152,128]{1,0:T(8,128)} %bitcast.30, f32[1152,128]{1,0:T(8,128)} %bitcast.31), custom_call_target="tpu_custom_call" | custom-call | tf_op jit(solution)/shard_map/potential/pallas_call | solution.py:212
  70.8 10.3 %apply.4 = (bf16[8,4,1152,128]{3,2,1,0:T(8,128)(2,1)}, f32[8,128]{1,0:T(8,128)}) custom-call(bf16[8,4,1152,128]{3,2,1,0:T(8,128)(2,1)} %bitcast.24, f32[4,144,8,128]{3,2,1,0:T(8,128)} %potential.1.pot_ref, bf16[2,4,288,128]{3,2,1,0:T(8,128)(2,1)} %collective-permute-done.4.near_ref.refs_2_, bf16[2,4,288,128]{3,2,1,0:T(8,128)(2,1)} %collective-permute-done.5.far_ref.refs_3_), custom_call_target="tpu_custom_call" | custom-call | tf_op jit(solution)/shard_map/apply/pallas_call | solution.py:339
  81.1 6.0 %collective-permute-done.2.refs_2_.near_ref = bf16[2,4,288,128]{3,2,1,0:T(8,128)(2,1)S(1)} collective-permute-done((bf16[2,4,288,128]{3,2,1,0:T(8,128)(2,1)}, bf16[2,4,288,128]{3,2,1,0:T(8,128)(2,1)S(1)}, u32[]{:S(2)}, u32[]{:S(2)}) %collective-permute-start.2) | collective-permute-done | bytes 589856 | tf_op jit(solution)/shard_map/ppermute | solution.py:393
  87.1 0.8 copy-done
  87.9 2.4 %collective-permute-start.6 = (bf16[2,4,288,128]{3,2,1,0:T(8,128)(2,1)}, bf16[2,4,288,128]{3,2,1,0:T(8,128)(2,1)S(1)}, u32[]{:S(2)}, u32[]{:S(2)}) collective-permute-start(bf16[2,4,288,128]{3,2,1,0:T(8,128)(2,1)} %get-tuple-element.31), channel_id=1, source_target_pairs={{0,1},{1,0},{2,3},{3,2},{4,5},{5,4},{6,7},{7,6},{8,9},{9,8},{10,11... | collective-permute-start | bytes 1769480 | tf_op jit(solution)/shard_map/ppermute | solution.py:393
  90.3 1.5 %collective-permute-start.7 = (bf16[2,4,288,128]{3,2,1,0:T(8,128)(2,1)}, bf16[2,4,288,128]{3,2,1,0:T(8,128)(2,1)}, u32[]{:S(2)}, u32[]{:S(2)}) collective-permute-start(bf16[2,4,288,128]{3,2,1,0:T(8,128)(2,1)} %get-tuple-element.32), channel_id=1, source_target_pairs={{1,2},{2,1},{3,4},{4,3},{5,6},{6,5},{9,10},{10,9},{11,12},{12,11},... | collective-permute-start | bytes 1769480 | tf_op jit(solution)/shard_map/ppermute | solution.py:393
  91.8 10.3 %apply.5 = (bf16[8,4,1152,128]{3,2,1,0:T(8,128)(2,1)}, f32[8,128]{1,0:T(8,128)}) custom-call(bf16[8,4,1152,128]{3,2,1,0:T(8,128)(2,1)} %bitcast.25, f32[4,144,8,128]{3,2,1,0:T(8,128)} %potential.1.pot_ref, bf16[2,4,288,128]{3,2,1,0:T(8,128)(2,1)} %copy-done, ...), custom_call_target="tpu_custom_call", output_to_operand_aliasing={{0}: (4, {})} | custom-call | tf_op jit(solution)/shard_map/apply/pallas_call | solution.py:339
  102.1 10.2 %collective-permute-done.8.near_ref = bf16[2,4,288,128]{3,2,1,0:T(8,128)(2,1)} collective-permute-done((bf16[2,4,288,128]{3,2,1,0:T(8,128)(2,1)}, bf16[2,4,288,128]{3,2,1,0:T(8,128)(2,1)}, u32[]{:S(2)}, u32[]{:S(2)}) %collective-permute-start.8) | collective-permute-done | bytes 589856 | tf_op jit(solution)/shard_map/ppermute | solution.py:393
  112.4 10.3 %apply.6 = (bf16[8,4,1152,128]{3,2,1,0:T(8,128)(2,1)}, f32[8,128]{1,0:T(8,128)}) custom-call(bf16[8,4,1152,128]{3,2,1,0:T(8,128)(2,1)} %bitcast.26, f32[4,144,8,128]{3,2,1,0:T(8,128)} %potential.1.pot_ref, bf16[2,4,288,128]{3,2,1,0:T(8,128)(2,1)} %collective-permute-done.8.near_ref, ...), custom_call_target="tpu_custom_call", output_to_operand_aliasing={{0}: (4, {})} | custom-call | tf_op jit(solution)/shard_map/apply/pallas_call | solution.py:339
  122.7 1.2 collective-permute-done.6.near_ref
  123.9 0.8 copy-done.1
  124.7 10.3 %apply.7 = (bf16[8,4,1152,128]{3,2,1,0:T(8,128)(2,1)}, f32[8,128]{1,0:T(8,128)}) custom-call(bf16[8,4,1152,128]{3,2,1,0:T(8,128)(2,1)} %bitcast.27, f32[4,144,8,128]{3,2,1,0:T(8,128)} %potential.1.pot_ref, bf16[2,4,288,128]{3,2,1,0:T(8,128)(2,1)} %copy-done.1, ...), custom_call_target="tpu_custom_call", output_to_operand_aliasing={{0}: (4, {})} | custom-call | tf_op jit(solution)/shard_map/apply/pallas_call | solution.py:339
  (9 shorter events, 0.0 us)
Async XLA Ops:
  11.8 3.3 %collective-permute-start = (bf16[4,1152,128]{2,1,0:T(8,128)(2,1)}, bf16[4,1152,128]{2,1,0:T(8,128)(2,1)}, u32[]{:S(2)}, u32[]{:S(2)}) collective-permute-start(bf16[4,1152,128]{2,1,0:T(8,128)(2,1)} %bitcast.28), channel_id=1, source_target_pairs={{0,8},{8,0},{16,24},{24,16},{1,9},{9,1},{17,25},{25,17},{2,10},{10... | collective-permute-start | bytes 3538952 | tf_op jit(solution)/shard_map/ppermute | solution.py:375
  18.1 47.7 %collective-permute-start.1 = (bf16[4,1152,128]{2,1,0:T(8,128)(2,1)}, bf16[4,1152,128]{2,1,0:T(8,128)(2,1)}, u32[]{:S(2)}, u32[]{:S(2)}) collective-permute-start(bf16[4,1152,128]{2,1,0:T(8,128)(2,1)} %add.1.d_ref), channel_id=1, source_target_pairs={{0,16},{8,24},{16,0},{24,8},{1,17},{9,25},{17,1},{25,9},{2,18},{10... | collective-permute-start | bytes 3538952 | tf_op jit(solution)/shard_map/ppermute | solution.py:375
  21.0 40.8 %collective-permute-start.4 = (bf16[2,4,288,128]{3,2,1,0:T(8,128)(2,1)}, bf16[2,4,288,128]{3,2,1,0:T(8,128)(2,1)}, u32[]{:S(2)}, u32[]{:S(2)}) collective-permute-start(bf16[2,4,288,128]{3,2,1,0:T(8,128)(2,1)} %get-tuple-element.28), channel_id=1, source_target_pairs={{0,1},{1,0},{2,3},{3,2},{4,5},{5,4},{6,7},{7,6},{8,9},{9,8},{10,11... | collective-permute-start | bytes 1769480 | tf_op jit(solution)/shard_map/ppermute | solution.py:393
  22.5 39.3 %collective-permute-start.5 = (bf16[2,4,288,128]{3,2,1,0:T(8,128)(2,1)}, bf16[2,4,288,128]{3,2,1,0:T(8,128)(2,1)}, u32[]{:S(2)}, u32[]{:S(2)}) collective-permute-start(bf16[2,4,288,128]{3,2,1,0:T(8,128)(2,1)} %get-tuple-element.29), channel_id=1, source_target_pairs={{1,2},{2,1},{3,4},{4,3},{5,6},{6,5},{9,10},{10,9},{11,12},{12,11},... | collective-permute-start | bytes 1769480 | tf_op jit(solution)/shard_map/ppermute | solution.py:393
  24.0 63.1 %collective-permute-start.2 = (bf16[2,4,288,128]{3,2,1,0:T(8,128)(2,1)}, bf16[2,4,288,128]{3,2,1,0:T(8,128)(2,1)S(1)}, u32[]{:S(2)}, u32[]{:S(2)}) collective-permute-start(bf16[2,4,288,128]{3,2,1,0:T(8,128)(2,1)} %get-tuple-element.26), channel_id=1, source_target_pairs={{0,1},{1,0},{2,3},{3,2},{4,5},{5,4},{6,7},{7,6},{8,9},{9,8},{10,11... | collective-permute-start | bytes 1769480 | tf_op jit(solution)/shard_map/ppermute | solution.py:393
  27.5 59.6 %collective-permute-start.3 = (bf16[2,4,288,128]{3,2,1,0:T(8,128)(2,1)}, bf16[2,4,288,128]{3,2,1,0:T(8,128)(2,1)}, u32[]{:S(2)}, u32[]{:S(2)}) collective-permute-start(bf16[2,4,288,128]{3,2,1,0:T(8,128)(2,1)} %get-tuple-element.27), channel_id=1, source_target_pairs={{1,2},{2,1},{3,4},{4,3},{5,6},{6,5},{9,10},{10,9},{11,12},{12,11},... | collective-permute-start | bytes 1769480 | tf_op jit(solution)/shard_map/ppermute | solution.py:393
  61.8 50.6 %collective-permute-start.8 = (bf16[2,4,288,128]{3,2,1,0:T(8,128)(2,1)}, bf16[2,4,288,128]{3,2,1,0:T(8,128)(2,1)}, u32[]{:S(2)}, u32[]{:S(2)}) collective-permute-start(bf16[2,4,288,128]{3,2,1,0:T(8,128)(2,1)} %get-tuple-element.35), channel_id=1, source_target_pairs={{0,1},{1,0},{2,3},{3,2},{4,5},{5,4},{6,7},{7,6},{8,9},{9,8},{10,11... | collective-permute-start | bytes 1769480 | tf_op jit(solution)/shard_map/ppermute | solution.py:393
  64.3 48.1 %collective-permute-start.9 = (bf16[2,4,288,128]{3,2,1,0:T(8,128)(2,1)}, bf16[2,4,288,128]{3,2,1,0:T(8,128)(2,1)}, u32[]{:S(2)}, u32[]{:S(2)}) collective-permute-start(bf16[2,4,288,128]{3,2,1,0:T(8,128)(2,1)} %get-tuple-element.36), channel_id=1, source_target_pairs={{1,2},{2,1},{3,4},{4,3},{5,6},{6,5},{9,10},{10,9},{11,12},{12,11},... | collective-permute-start | bytes 1769480 | tf_op jit(solution)/shard_map/ppermute | solution.py:393
  87.1 0.8 copy-start
  87.9 36.0 %collective-permute-start.6 = (bf16[2,4,288,128]{3,2,1,0:T(8,128)(2,1)}, bf16[2,4,288,128]{3,2,1,0:T(8,128)(2,1)S(1)}, u32[]{:S(2)}, u32[]{:S(2)}) collective-permute-start(bf16[2,4,288,128]{3,2,1,0:T(8,128)(2,1)} %get-tuple-element.31), channel_id=1, source_target_pairs={{0,1},{1,0},{2,3},{3,2},{4,5},{5,4},{6,7},{7,6},{8,9},{9,8},{10,11... | collective-permute-start | bytes 1769480 | tf_op jit(solution)/shard_map/ppermute | solution.py:393
  90.3 33.6 %collective-permute-start.7 = (bf16[2,4,288,128]{3,2,1,0:T(8,128)(2,1)}, bf16[2,4,288,128]{3,2,1,0:T(8,128)(2,1)}, u32[]{:S(2)}, u32[]{:S(2)}) collective-permute-start(bf16[2,4,288,128]{3,2,1,0:T(8,128)(2,1)} %get-tuple-element.32), channel_id=1, source_target_pairs={{1,2},{2,1},{3,4},{4,3},{5,6},{6,5},{9,10},{10,9},{11,12},{12,11},... | collective-permute-start | bytes 1769480 | tf_op jit(solution)/shard_map/ppermute | solution.py:393
  123.9 0.8 copy-start.1
